TPU v7x, 256 devices: a whole 4x4x8 slice. The times are simulated.
256 devices in a mesh: sec: 16 (over y, x), term: 16 (over z, core).
Axes of the slice: x: 4, y: 4, z: 8, core: 2. Of those that a mesh axis runs over, the one named last changes fastest.
Arguments:
- psi: bfloat16 [128, 384, 384], P('sec'), may hold values from -6 to 6
- left_env: bfloat16 [16, 2, 128, 384, 384], P('term', None, 'sec'), may hold values from -0.3125 to 0.3125
- right_env: bfloat16 [16, 2, 128, 384, 384], P('term', None, 'sec'), may hold values from -0.21875 to 0.21875
- targets: int32 [16, 128], P('term', 'sec'), may hold values from 0 to 127, as said below
- selected: int32 [16, 128], P('term', 'sec'), may hold values from 0 to 1, as said below
- block_dims: int32 [128, 2], P('sec'), may hold values from 192 to 384, as said below
Outputs:
- sigma: bfloat16 [128, 384, 384], P('sec', 'term')
Inputs may be any that keep to these rules, and one draw needn't show every extreme that they name: For each term class w, targets[w] is a permutation of the 128 blocks. Blocks k and k2 belong to the same index of sec when k // 8 = k2 // 8; under one term class the blocks of one index of sec go to exactly 8 distinct indices of sec, exactly 1 block to each. Under each term class, between 1 and 6 of the 8 blocks of one index of sec are selected, exactly 6 on some index. `block_dims`: some block has both dimensions equal to 384.
All inputs are finite; a program needn't handle non-finite values.
Results may differ from a plain program's by a relative error of at most 0.013.
Values may be sent and summed in bfloat16 or wider, within the bound.
A program may use at most 64 MiB of HBM per device.

v0:
```python
import jax
import jax.numpy as jnp
from jax import lax
from jax.sharding import PartitionSpec as P


def in_blocks(shard, dim, peers):
    lengths = shard.shape
    pieces = shard.reshape(*lengths[:dim], peers, lengths[dim] // peers, *lengths[dim + 1 :])
    return jnp.moveaxis(pieces, dim, 0)


def in_order(pieces, dim):
    lengths = list(pieces.shape[1:])
    lengths[dim] *= pieces.shape[0]
    return jnp.moveaxis(pieces, 0, dim).reshape(lengths)


def one_exchange(shard, axis, axes, splits, concats):
    sizes = [lax.axis_size(a) for a in axes]
    pieces = in_blocks(shard, splits[0], sizes[0])
    pieces = jnp.moveaxis(in_blocks(pieces, splits[1] + 1, sizes[1]), 0, 1)
    inside = pieces.shape[2:]
    pieces = pieces.reshape(-1, *inside)
    pieces = lax.all_to_all(pieces, axis, split_axis=0, concat_axis=0, tiled=True)
    pieces = in_order(pieces.reshape(*sizes, *inside), concats[0] + 1)
    return in_order(pieces, concats[1])


def shards(psi, left_env, right_env, targets, selected, block_dims):
    sec_count = lax.axis_size("sec")
    term_count = lax.axis_size("term")
    blocks_here = psi.shape[0]
    block_width = psi.shape[1]
    capacity = blocks_here // min(blocks_here, sec_count)
    positions = jnp.arange(block_width, dtype=jnp.int32)
    rows_ok = positions[None, :] < block_dims[:, 0:1]
    cols_ok = positions[None, :] < block_dims[:, 1:2]
    inside = rows_ok[:, :, None] & cols_ok[:, None, :]
    masked = jnp.where(inside, psi, jnp.zeros_like(psi))
    target_row = targets[0]
    chosen_row = selected[0]
    left_blocks = left_env[0]
    right_blocks = right_env[0]
    half_product = jnp.einsum(
        "mkab,kbc->mkac", left_blocks, masked, preferred_element_type=jnp.float32
    ).astype(jnp.bfloat16)
    result_blocks = jnp.einsum(
        "mkab,mkbc->kac", half_product, right_blocks, preferred_element_type=jnp.float32
    )
    result_blocks = (result_blocks * chosen_row.astype(jnp.float32)[:, None, None]).astype(
        jnp.bfloat16
    )
    owners = target_row // blocks_here
    local_slot = target_row % blocks_here
    item_count = owners.shape[0]
    same_owner = owners[:, None] == owners[None, :]
    earlier = jnp.arange(item_count)[None, :] < jnp.arange(item_count)[:, None]
    slot_rank = jnp.sum((same_owner & earlier).astype(jnp.int32), axis=1)
    send_slot = owners * capacity + slot_rank
    slot_total = sec_count * capacity
    placing = send_slot[None, :] == jnp.arange(slot_total, dtype=jnp.int32)[:, None]
    slot_ids = jnp.sum(jnp.where(placing, local_slot[None, :] + 1, 0), axis=1) - 1
    slot_ids = slot_ids.reshape(sec_count, capacity)
    row_count = block_width // term_count
    place_grid = placing.astype(jnp.bfloat16).reshape(sec_count, capacity, item_count)
    banded = result_blocks.reshape(item_count, term_count, row_count, block_width)
    outgoing = jnp.einsum(
        "sck,ktab->stcab", place_grid, banded, preferred_element_type=jnp.float32
    ).astype(jnp.bfloat16)
    stripe_ids = jnp.broadcast_to(slot_ids[:, None, :], (sec_count, term_count, capacity))
    arrived, arrived_ids = (
        one_exchange(outgoing, ("sec", "term"), ("sec", "term"), (0, 1), (0, 1)),
        one_exchange(stripe_ids, ("sec", "term"), ("sec", "term"), (0, 1), (0, 1)),
    )
    incoming = sec_count * term_count * capacity
    landing = arrived_ids.reshape(-1)[None, :] == jnp.arange(blocks_here, dtype=jnp.int32)[:, None]
    summed = jnp.einsum(
        "js,sab->jab",
        landing.astype(jnp.bfloat16),
        arrived.reshape(incoming, row_count, block_width),
        preferred_element_type=jnp.float32,
    )
    row_ids = lax.axis_index("term") * row_count + jnp.arange(row_count, dtype=jnp.int32)
    rows_mine = row_ids[None, :] < block_dims[:, 0:1]
    keep_mine = rows_mine[:, :, None] & cols_ok[:, None, :]
    return jnp.where(keep_mine, summed, jnp.zeros_like(summed)).astype(jnp.bfloat16)


def solution(mesh):
    return jax.shard_map(
        shards,
        mesh=mesh,
        in_specs=(
            P("sec", None, None),
            P("term", None, "sec", None, None),
            P("term", None, "sec", None, None),
            P("term", "sec"),
            P("term", "sec"),
            P("sec", None),
        ),
        out_specs=P("sec", "term", None),
        check_vma=False,
    )
```

profile of v0, /device:TPU:1, one launch (start us, length us, event | category | flops | bytes accessed | tf_op | source)
XLA Modules:
  0.0 163.2 jit_solution(1147862907733701710)
XLA Ops:
  0.0 0.7 fusion.35
  0.7 0.7 and_select_fusion.2
  1.3 0.2 convert_reduce_fusion
  1.5 0.1 select_reduce_fusion
  1.6 0.1 broadcast_in_dim.25
  1.7 0.9 broadcast_in_dim.50
  2.6 15.7 %all-to-all-start = ((s32[256,1,1,1]{3,2,1,0:T(1,128)}), s32[256,1,1,1]{3,2,1,0:T(1,128)S(1)}, u32[]{:S(2)}, u32[]{:S(2)}) async-start(s32[256,1,1,1]{3,2,1,0:T(1,128)} %broadcast_in_dim.50), calls=%async_computation | async-start | bytes 262144 | tf_op jit(solution)/shard_map/all_to_all | solution.py:25
  18.3 0.8 slice_bitcast_fusion.1
  19.0 0.7 convert_bitcast_fusion.1
  19.7 0.1 iota_compare_fusion
  19.8 8.8 %fusion = bf16[8,384,384]{2,1,0:T(8,128)(2,1)S(1)} fusion(f32[8]{0:T(128)S(1)} %convert_bitcast_fusion.1, bf16[8,384,384]{2,1,0:T(8,128)(2,1)} %param.6, pred[8,384]{1,0:T(8,128)(4,1)S(1)} %get-tuple-element.10, pred[8,384]{1,0:T(8,128)(4,1)S(1)} %get-tuple-element.9, bf16[1,2,8,384,384]{4,3,2,1,0:T(8,128)(2,1)} %param.8, bf16[1,2,8,384,384]{4,3,2,1,0:T(8,128)(2,1)} %param.7), kind=kOutput, calls=%fused_computation.1 | convolution fusion | flops 3630956544 | bytes 14161952 | tf_op jit(solution)/shard_map/mkab,mkbc->kac/dot_general | solution.py:48
  28.6 1.9 %convert_bitcast_fusion = bf16[16,16,1,24,384]{4,0,3,1,2:T(8,128)(2,1)S(1)} fusion(bf16[8,16,24,384]{3,2,1,0:T(8,128)(2,1)S(1)} %bitcast.88, s32[8]{0:T(128)S(1)} %fusion.36), kind=kOutput, calls=%fused_computation.7 | convolution fusion | flops 40108160 | bytes 7077920 | tf_op jit(solution)/shard_map/sck,ktab->stcab/dot_general | solution.py:68
  30.5 3.3 %copy.54 = bf16[16,16,1,24,384]{4,3,1,0,2:T(8,128)(2,1)} copy(bf16[16,16,1,24,384]{4,0,3,1,2:T(8,128)(2,1)S(1)} %convert_bitcast_fusion) | data formatting | bytes 9437184 | tf_op jit(solution)/shard_map/convert_element_type | solution.py:70
  33.8 0.0 all-to-all-done
  33.8 14.6 %all-to-all-start.1 = ((bf16[256,1,1,1,24,384]{5,4,3,2,1,0:T(8,128)(2,1)}), bf16[256,1,1,1,24,384]{5,4,3,2,1,0:T(8,128)(2,1)}, u32[]{:S(2)}, u32[]{:S(2)}) async-start(bf16[256,1,1,1,24,384]{5,4,3,2,1,0:T(8,128)(2,1)} %bitcast.86), calls=%async_computation.1 | async-start | bytes 9437184 | tf_op jit(solution)/shard_map/all_to_all | solution.py:25
  48.4 0.1 broadcast_compare_fusion
  48.5 4.6 %reduce = s32[256]{0:T(256)S(1)} reduce(s32[256,1,1,1]{3,2,1,0:T(1,128)S(1)} %all-to-all-done, s32[]{:T(128)} %constant.35.clone.1), dimensions={1,2,3}, to_apply=%all_to_all.6.reduce_sub_computation | reduce | bytes 2052 | tf_op jit(solution)/shard_map/all_to_all | solution.py:25
  53.1 0.1 reshape.181
  53.2 0.1 copy.47
  53.3 0.1 copy.48
  53.4 0.1 eq.78
  53.4 105.1 %all-to-all-done.1 = bf16[256,1,1,1,24,384]{5,4,3,2,1,0:T(8,128)(2,1)} async-done(((bf16[256,1,1,1,24,384]{5,4,3,2,1,0:T(8,128)(2,1)}), bf16[256,1,1,1,24,384]{5,4,3,2,1,0:T(8,128)(2,1)}, u32[]{:S(2)}, u32[]{:S(2)}) %all-to-all-start.1) | async-done | bytes 4718624 | tf_op jit(solution)/shard_map/all_to_all | solution.py:25
  158.6 3.2 %copy.56 = bf16[16,16,1,1,1,24,384]{6,1,0,5,4,3,2:T(8,128)(2,1)S(1)} copy(bf16[16,16,1,1,1,24,384]{6,5,1,0,4,3,2:T(8,128)(2,1)} %bitcast.26) | data formatting | bytes 9437184 | tf_op jit(solution)/shard_map/reshape | solution.py:26
  161.8 0.7 fusion.26
  162.5 0.7 copy.57
  (3 shorter events, 0.0 us)
Async XLA Ops:
  2.6 31.2 %all-to-all-start = ((s32[256,1,1,1]{3,2,1,0:T(1,128)}), s32[256,1,1,1]{3,2,1,0:T(1,128)S(1)}, u32[]{:S(2)}, u32[]{:S(2)}) async-start(s32[256,1,1,1]{3,2,1,0:T(1,128)} %broadcast_in_dim.50), calls=%async_computation | async-start | bytes 262144 | tf_op jit(solution)/shard_map/all_to_all | solution.py:25
  33.8 124.8 %all-to-all-start.1 = ((bf16[256,1,1,1,24,384]{5,4,3,2,1,0:T(8,128)(2,1)}), bf16[256,1,1,1,24,384]{5,4,3,2,1,0:T(8,128)(2,1)}, u32[]{:S(2)}, u32[]{:S(2)}) async-start(bf16[256,1,1,1,24,384]{5,4,3,2,1,0:T(8,128)(2,1)} %bitcast.86), calls=%async_computation.1 | async-start | bytes 9437184 | tf_op jit(solution)/shard_map/all_to_all | solution.py:25
where the time goes:
time: 163 us
  waiting for transfers between devices  105 us (64%)
  starting transfers between devices  30.3 us (19%)
  matrix products  11.5 us (7%)
  local copies, waits for them, and re-layouts  9.22 us (6%)
  other arithmetic  7.04 us (4%)
    all_to_all x2, waiting for transfers between devices, one_exchange(): lax.all_to_all(pieces, axis, split_axis=0, concat_axis=0, tiled=True)  105 us
    all_to_all x2, starting transfers between devices, one_exchange(): lax.all_to_all(pieces, axis, split_axis=0, concat_axis=0, tiled=True)  30.3 us
    dot_general x1, matrix products, shards(): jnp.einsum('mkab,mkbc->kac', half_product, right_blocks, preferred_elemen...  8.82 us
    all_to_all x1, other arithmetic, one_exchange(): lax.all_to_all(pieces, axis, split_axis=0, concat_axis=0, tiled=True)  4.62 us
    convert_element_type x1, local copies, waits for them, and re-layouts, shards(): outgoing = jnp.einsum('sck,ktab->stcab', place_grid, banded, preferred_el...  3.32 us
  transfers between devices with their start and end apart: 2, of which 1 were waited for; matrix products, arithmetic and copies ran while one was open for 13% of the time, Pallas kernels for 0%

commit v1 on v0

v1 whole, which is shorter than its diff:
```python
import functools
import math

import jax
import jax.numpy as jnp
from jax import lax
from jax.experimental import pallas as pl
from jax.experimental.pallas import tpu as pltpu
from jax.sharding import PartitionSpec as P

MESH = pl.DeviceIdType.MESH
ITEMS = 6
COLS = 128
SUB = 8


def kernel(
    W, NY, NX,
    tgt, sel, dims, psi_h, left_h, right_h, out,
    psi_v, left_v, right_v, zsend, zrecv, msend, mrecv, onehot, ybuf,
    a1, b1, a2s, b2s, a2, b2, fin,
    load_sem, mesh_sems, zs_sem, zr_sem, s1_sem, r1_sem, s2_sem, r2_sem,
):
    w = lax.axis_index("term")
    s = lax.axis_index("sec")
    y, x = s // NX, s % NX
    NB, BS = psi_v.shape[0], psi_v.shape[1]
    C = BS // COLS
    rows = BS // W
    G = rows // SUB
    L = G * COLS
    R6 = ITEMS * SUB
    half = NB * SUB // 2
    pairs = ITEMS // 2
    K = W * R6

    loads = [(psi_h, psi_v)]
    for m in range(2):
        loads.append((left_h.at[0, m], left_v.at[m]))
        loads.append((right_h.at[0, m], right_v.at[m]))
    loads = [pltpu.make_async_copy(a, b, load_sem.at[n]) for n, (a, b) in enumerate(loads)]
    for copy in loads:
        copy.start()

    def z_peer(d):
        return lax.rem(w + d, W)

    def sec_at(yy, xx):
        return yy * NX + xx

    barrier = pltpu.get_barrier_semaphore()

    def greet(d, carry):
        pl.semaphore_signal(barrier, inc=1, device_id={"term": z_peer(d)}, device_id_type=MESH)
        return carry

    lax.fori_loop(1, W, greet, 0)
    for d in range(1, NY):
        pl.semaphore_signal(
            barrier, inc=1, device_id={"sec": sec_at(lax.rem(y + d, NY), x)}, device_id_type=MESH)
    for d in range(1, NX):
        pl.semaphore_signal(
            barrier, inc=1, device_id={"sec": sec_at(y, lax.rem(x + d, NX))}, device_id_type=MESH)

    chosen, ranks, count = [], [], jnp.int32(0)
    for k in range(NB):
        chosen.append(sel[0, k] != 0)
        ranks.append(count)
        count = count + jnp.where(chosen[k], 1, 0)

    def block_of(i):
        found = jnp.int32(0)
        for k in range(NB):
            found = found + jnp.where(chosen[k] & (ranks[k] == i), k, 0)
        return found

    lane = lax.broadcasted_iota(jnp.int32, (1, 128), 1)
    message = jnp.zeros((1, 128), jnp.int32)
    for i in range(ITEMS):
        place = jnp.int32(-1)
        for k in range(NB):
            place = place + jnp.where(chosen[k] & (ranks[k] == i), tgt[0, k] + 1, 0)
        value = jnp.where(place >= 0, place * SUB + lane % SUB + 1, 0)
        message = jnp.where(lane // SUB == i, value, message)
    msend[...] = message
    mrecv[w] = message

    pl.semaphore_wait(barrier, W - 1 + NY - 1 + NX - 1)

    def send_message(d, carry):
        pltpu.make_async_remote_copy(
            msend, mrecv.at[w], mesh_sems.at[0], mesh_sems.at[1],
            device_id={"term": z_peer(d)}, device_id_type=MESH).start()
        return carry

    lax.fori_loop(1, W, send_message, 0)

    def send_z(c, first, size, piece):
        part = pl.ds(first, size)

        def one(d, carry):
            peer = z_peer(d)
            pltpu.make_async_remote_copy(
                zsend.at[c, peer, part], zrecv.at[c, w, part], zs_sem.at[piece], zr_sem.at[piece],
                device_id={"term": peer}, device_id_type=MESH).start()
            return carry

        lax.fori_loop(1, W, one, 0)

    def wait_for(ref, sem):
        pltpu.make_async_copy(ref, ref, sem).wait()

    for copy in loads:
        copy.wait()

    row_id = lax.broadcasted_iota(jnp.int32, (BS, BS), 0)
    col_id = lax.broadcasted_iota(jnp.int32, (BS, BS), 1)

    def one_block(i):
        k = block_of(i)
        block = psi_v[k]
        keep = (row_id < dims[k, 0]) & (col_id < dims[k, 1])
        block = jnp.where(keep, block, jnp.zeros_like(block))
        total = None
        for m in range(2):
            half_product = jnp.dot(left_v[m, k], block, preferred_element_type=jnp.float32)
            term = jnp.dot(
                half_product.astype(jnp.bfloat16), right_v[m, k], preferred_element_type=jnp.float32)
            total = term if total is None else total + term
        return total.reshape(W * G, SUB, BS)

    def one_pair(p, carry):
        both = jnp.concatenate([one_block(2 * p), one_block(2 * p + 1)], axis=1).astype(jnp.bfloat16)
        both = both.reshape(W, G, 2 * SUB, BS)
        first = pl.multiple_of(p * 2 * SUB, 2 * SUB)
        for c in range(C):
            for g in range(G):
                zsend[c, :, pl.ds(first, 2 * SUB), g * COLS:(g + 1) * COLS] = (
                    both[:, g, :, c * COLS:(c + 1) * COLS])
        send_z(0, first, 2 * SUB, p)
        return carry

    lax.fori_loop(0, pairs, one_pair, 0)
    for c in range(1, C):
        send_z(c, 0, R6, pairs - 1 + c)
    for c in range(C):
        zrecv[c, w] = zsend[c, w]

    wait_for(mrecv.at[pl.ds(0, W - 1)], mesh_sems.at[1])
    width = -(-K // 128) * 128
    places = jnp.zeros((2 * SUB, width), jnp.int32)
    for n in range(W):
        wide = jnp.broadcast_to(mrecv[n], (2 * SUB, 128))
        if width > 128:
            wide = jnp.concatenate([wide, jnp.zeros((2 * SUB, width - 128), jnp.int32)], axis=1)
        places = places + (pltpu.roll(wide, n * R6, 1) if n else wide)
    places = places[:, :K]
    step = lax.broadcasted_iota(jnp.int32, (2 * SUB, K), 0) + 1

    def fill(b, carry):
        first = pl.multiple_of(b * 2 * SUB, 2 * SUB)
        onehot[pl.ds(first, 2 * SUB), :] = jnp.where(
            places == step + first, 1.0, 0.0).astype(jnp.bfloat16)
        return carry

    lax.fori_loop(0, NY * NX * NB * SUB // (2 * SUB), fill, 0)

    block_rows = NX * NB * SUB
    for c in range(C):
        if c == 0:
            for p in range(pairs):
                wait_for(zrecv.at[0, pl.ds(0, W - 1), pl.ds(p * 2 * SUB, 2 * SUB)], zr_sem.at[p])
        else:
            wait_for(zrecv.at[c, pl.ds(0, W - 1)], zr_sem.at[pairs - 1 + c])
        arrived = zrecv[c].reshape(K, L)
        for yy in range(NY):
            part = jnp.dot(
                onehot[yy * block_rows:(yy + 1) * block_rows, :], arrived,
                preferred_element_type=jnp.float32)
            ybuf[c, yy] = part.astype(jnp.bfloat16).reshape(NX, NB * SUB, L)
        for d in range(1, NY):
            yy = lax.rem(y + d, NY)
            pltpu.make_async_remote_copy(
                ybuf.at[c, yy, :, pl.ds(0, half)], a1.at[c, d - 1], s1_sem.at[0, c], r1_sem.at[0, c],
                device_id={"sec": sec_at(yy, x)}, device_id_type=MESH).start()
        for d in range(1, NX):
            xx = lax.rem(x + d, NX)
            pltpu.make_async_remote_copy(
                ybuf.at[c, :, xx, pl.ds(half, half)], b1.at[c, d - 1], s1_sem.at[1, c], r1_sem.at[1, c],
                device_id={"sec": sec_at(y, xx)}, device_id_type=MESH).start()

        wait_for(a1.at[c], r1_sem.at[0, c])
        total = ybuf[c, y, :, :half, :].astype(jnp.float32)
        for n in range(NY - 1):
            total = total + a1[c, n].astype(jnp.float32)
        a2s[c] = total.astype(jnp.bfloat16)
        for d in range(1, NX):
            xx = lax.rem(x + d, NX)
            pltpu.make_async_remote_copy(
                a2s.at[c, xx], a2.at[c, d - 1], s2_sem.at[0, c], r2_sem.at[0, c],
                device_id={"sec": sec_at(y, xx)}, device_id_type=MESH).start()
        wait_for(b1.at[c], r1_sem.at[1, c])
        total = ybuf[c, :, x, half:, :].astype(jnp.float32)
        for n in range(NX - 1):
            total = total + b1[c, n].astype(jnp.float32)
        b2s[c] = total.astype(jnp.bfloat16)
        for d in range(1, NY):
            yy = lax.rem(y + d, NY)
            pltpu.make_async_remote_copy(
                b2s.at[c, yy], b2.at[c, d - 1], s2_sem.at[1, c], r2_sem.at[1, c],
                device_id={"sec": sec_at(yy, x)}, device_id_type=MESH).start()

        wait_for(a2.at[c], r2_sem.at[0, c])
        wait_for(b2.at[c], r2_sem.at[1, c])
        for own, others, place, at in ((a2s, a2, x, 0), (b2s, b2, y, NB // 2)):
            total = own[c, place].astype(jnp.float32)
            for n in range(others.shape[1]):
                total = total + others[c, n].astype(jnp.float32)
            for g in range(G):
                fin[at:at + NB // 2, g * SUB:(g + 1) * SUB, c * COLS:(c + 1) * COLS] = (
                    total[:, g * COLS:(g + 1) * COLS].reshape(NB // 2, SUB, COLS))

    row_id = lax.broadcasted_iota(jnp.int32, (rows, BS), 0) + w * rows
    col_id = lax.broadcasted_iota(jnp.int32, (rows, BS), 1)
    for j in range(NB):
        keep = (row_id < dims[j, 0]) & (col_id < dims[j, 1])
        out[j] = jnp.where(keep, fin[j], 0.0).astype(out.dtype)

    for _ in range(1):
        wait_for(mrecv.at[pl.ds(0, W - 1)], mesh_sems.at[0])
    for p in range(pairs):
        wait_for(zsend.at[0, pl.ds(0, W - 1), pl.ds(p * 2 * SUB, 2 * SUB)], zs_sem.at[p])
    for c in range(1, C):
        wait_for(zsend.at[c, pl.ds(0, W - 1)], zs_sem.at[pairs - 1 + c])
    for c in range(C):
        wait_for(a1.at[c], s1_sem.at[0, c])
        wait_for(b1.at[c], s1_sem.at[1, c])
        wait_for(a2.at[c], s2_sem.at[0, c])
        wait_for(b2.at[c], s2_sem.at[1, c])


def shards(W, SEC, psi, left_env, right_env, targets, selected, block_dims):
    NB, BS, _ = psi.shape
    NX = math.isqrt(SEC)
    NY = SEC // NX
    C = BS // COLS
    rows = BS // W
    G = rows // SUB
    L = G * COLS
    R6 = ITEMS * SUB
    half = NB * SUB // 2
    bf16, f32, i32 = jnp.bfloat16, jnp.float32, jnp.int32
    dma = pltpu.SemaphoreType.DMA
    smem = pl.BlockSpec(memory_space=pltpu.SMEM)
    anyspace = pl.BlockSpec(memory_space=pl.ANY)
    pieces = ITEMS // 2 + C - 1
    return pl.pallas_call(
        functools.partial(kernel, W, NY, NX),
        out_shape=jax.ShapeDtypeStruct((NB, rows, BS), bf16),
        in_specs=[smem, smem, smem, anyspace, anyspace, anyspace],
        out_specs=pl.BlockSpec(memory_space=pltpu.VMEM),
        scratch_shapes=[
            pltpu.VMEM((NB, BS, BS), bf16),
            pltpu.VMEM((2, NB, BS, BS), bf16),
            pltpu.VMEM((2, NB, BS, BS), bf16),
            pltpu.VMEM((C, W, R6, L), bf16),
            pltpu.VMEM((C, W, R6, L), bf16),
            pltpu.VMEM((1, 128), i32),
            pltpu.VMEM((W, 1, 128), i32),
            pltpu.VMEM((SEC * NB * SUB, W * R6), bf16),
            pltpu.VMEM((C, NY, NX, NB * SUB, L), bf16),
            pltpu.VMEM((C, NY - 1, NX, half, L), bf16),
            pltpu.VMEM((C, NX - 1, NY, half, L), bf16),
            pltpu.VMEM((C, NX, half, L), bf16),
            pltpu.VMEM((C, NY, half, L), bf16),
            pltpu.VMEM((C, NX - 1, half, L), bf16),
            pltpu.VMEM((C, NY - 1, half, L), bf16),
            pltpu.VMEM((NB, rows, BS), f32),
            dma((5,)), dma((2,)), dma((pieces,)), dma((pieces,)),
            dma((2, C)), dma((2, C)), dma((2, C)), dma((2, C)),
        ],
        compiler_params=pltpu.CompilerParams(
            collective_id=0, has_side_effects=True, vmem_limit_bytes=48 * 2**20),
        cost_estimate=pl.CostEstimate(flops=8 * 10**9, bytes_accessed=12 * 10**6, transcendentals=0),
        name="davidson",
    )(targets, selected, block_dims, psi, left_env, right_env)


def solution(mesh):
    W, SEC = mesh.shape["term"], mesh.shape["sec"]
    return jax.shard_map(
        functools.partial(shards, W, SEC),
        mesh=mesh,
        in_specs=(
            P("sec", None, None),
            P("term", None, "sec", None, None),
            P("term", None, "sec", None, None),
            P("term", "sec"),
            P("term", "sec"),
            P("sec", None),
        ),
        out_specs=P("sec", "term", None),
        check_vma=False,
    )
```

time: 163 us -> 69.6 us (0.43)
  waiting for transfers between devices: 105 us -> 0 us
  Pallas kernels: 0 us -> 65.1 us
  starting transfers between devices: 30.3 us -> 0 us
  matrix products: 11.5 us -> 0 us
  other arithmetic: 7.04 us -> 0 us
  local copies, waits for them, and re-layouts: 9.22 us -> 4.39 us
    all_to_all x2 -> x0, waiting for transfers between devices: 105 us -> none  [one_exchange(): lax.all_to_all(pieces, axis, split_axis=0, concat_axis=0, tiled=True)]
    pallas_call x0 -> x1, Pallas kernels: none -> 65.1 us  [shards(): pl.pallas_call(functools.partial(kernel, W, NY, NX), out_shape=jax.ShapeD...]
    all_to_all x2 -> x0, starting transfers between devices: 30.3 us -> none  [one_exchange(): lax.all_to_all(pieces, axis, split_axis=0, concat_axis=0, tiled=True)]
    dot_general x3 -> x0, matrix products: 11.5 us -> none  [the longest x1 8.82 us: shards(): jnp.einsum('mkab,mkbc->kac', half_product, right_blocks, preferred_elemen...]
    all_to_all x1 -> x0, other arithmetic: 4.62 us -> none  [one_exchange(): lax.all_to_all(pieces, axis, split_axis=0, concat_axis=0, tiled=True)]
    unnamed x0 -> x8, local copies, waits for them, and re-layouts: none -> 4.39 us
    convert_element_type x2 -> x0, local copies, waits for them, and re-layouts: 4 us -> none  [the longest x1 3.32 us: shards(): outgoing = jnp.einsum('sck,ktab->stcab', place_grid, banded, preferred_el...]
    reshape x2 -> x0, local copies, waits for them, and re-layouts: 3.25 us -> none  [one_exchange(): pieces = in_order(pieces.reshape(*sizes, *inside), concats[0] + 1)]
  transfers between devices with their start and end apart: 2 -> 0, of which waited for: 1 -> 0; matrix products, arithmetic and copies ran while one was open for 13% -> 0% of each run, Pallas kernels for 0% -> 0%
where the time goes in v1:
time: 69.6 us; the launch traced here: 69.5 us
  Pallas kernels  65.1 us (94%)
  local copies, waits for them, and re-layouts  4.39 us (6%)
    pallas_call x1, Pallas kernels, shards(): pl.pallas_call(functools.partial(kernel, W, NY, NX), out_shape=jax.ShapeD...  65.1 us
    unnamed x8, local copies, waits for them, and re-layouts  4.39 us

profile of v1, /device:TPU:1, one launch (start us, length us, event | category | flops | bytes accessed | tf_op | source)
XLA Modules:
  0.0 69.5 jit_solution(7084443618368556276)
XLA Ops:
  0.0 0.8 %copy.7.dims = s32[8,2]{1,0:T(8,128)S(1)} copy(s32[8,2]{0,1:T(2,128)} %param.11) | data formatting | bytes 128 | tf_op args[5]
  0.8 0.0 copy-start
  0.8 1.7 %copy-done = bf16[8,384,384]{2,1,0:T(8,128)(2,1)S(1)} copy-done((bf16[8,384,384]{2,1,0:T(8,128)(2,1)S(1)}, bf16[8,384,384]{2,1,0:T(8,128)(2,1)}, u32[]{:S(2)}) %copy-start) | copy-done | bytes 2359320
  2.4 0.0 copy-start.1
  2.4 0.7 copy-done.1
  3.1 0.0 copy-start.2
  3.1 0.7 copy-done.2
  3.7 65.1 %davidson.1 = bf16[8,24,384]{2,1,0:T(8,128)(2,1)S(1)} custom-call(s32[1,8]{1,0:T(1,128)S(1)} %copy-done.1, s32[1,8]{1,0:T(1,128)S(1)} %copy-done.2, s32[8,2]{1,0:T(8,128)S(1)} %copy.7.dims, bf16[8,384,384]{2,1,0:T(8,128)(2,1)S(1)} %copy-done, bf16[1,2,8,384,384]{4,3,2,1,0:T(8,128)(2,1)} %left_h.1, bf16[1,2,8,384,384]{4,3,2,1,0:T(8,128)(2,1)} %right_h.1), custom_call_target="tpu_custom_call" | custom-call | flops 8000000000 | bytes 12000000 | tf_op jit(solution)/shard_map/davidson/pallas_call | solution.py:257
  68.8 0.7 copy.9
Async XLA Ops:
  0.8 1.7 %copy-start = (bf16[8,384,384]{2,1,0:T(8,128)(2,1)S(1)}, bf16[8,384,384]{2,1,0:T(8,128)(2,1)}, u32[]{:S(2)}) copy-start(bf16[8,384,384]{2,1,0:T(8,128)(2,1)} %psi_h.1) | copy-start | bytes 7077892
  2.4 0.7 copy-start.1
  3.1 0.7 copy-start.2

commit v2 on v1

v2 whole, which is shorter than its diff:
```python
import functools
import math

import jax
import jax.numpy as jnp
from jax import lax
from jax.experimental import pallas as pl
from jax.experimental.pallas import tpu as pltpu
from jax.sharding import PartitionSpec as P

MESH = pl.DeviceIdType.MESH
ITEMS = 6
COLS = 128
SUB = 8
XG = 2


def kernel(
    W, NY, NX,
    tgt_h, sel_h, dims_h, psi_h, left_h, right_h, out,
    tgt, sel, dims, psi_v, left_v, right_v, zsend, zrecv, msend, mrecv, onehot, ybuf,
    a1, b1, a2s, b2s, a2, b2, fin,
    xmsend, xmrecv, xitems, xsend, xrecv, xhot, xplaced, xcore, xsum, xlast,
    int_sem, load_sem, mesh_sems, zs_sem, zr_sem, s1_sem, r1_sem, s2_sem, r2_sem, xs_sem, xr_sem,
):
    w = lax.axis_index("term")
    s = lax.axis_index("sec")
    y, x = s // NX, s % NX
    NB, BS = psi_v.shape[0], psi_v.shape[1]
    rows = BS // W
    G = rows // SUB
    C = BS // COLS * G - XG
    R6 = ITEMS * SUB
    half = NB * SUB // 2
    pairs = ITEMS // 2
    K = W * R6
    SEC = NY * NX
    z, core = w // 2, w % 2

    ints = [(tgt_h, tgt), (sel_h, sel), (dims_h, dims)]
    ints = [pltpu.make_async_copy(a, b, int_sem.at[n]) for n, (a, b) in enumerate(ints)]
    for copy in ints:
        copy.start()
    loads = [(psi_h, psi_v)]
    for m in range(2):
        loads.append((left_h.at[0, m], left_v.at[:, m]))
    for m in range(2):
        loads.append((right_h.at[0, m], right_v.at[:, m]))
    loads = [pltpu.make_async_copy(a, b, load_sem.at[n]) for n, (a, b) in enumerate(loads)]
    for copy in loads:
        copy.start()

    def z_peer(d):
        return lax.rem(w + d, W)

    def sec_at(yy, xx):
        return yy * NX + xx

    barrier = pltpu.get_barrier_semaphore()

    def greet(d, carry):
        pl.semaphore_signal(barrier, inc=1, device_id={"term": z_peer(d)}, device_id_type=MESH)
        return carry

    lax.fori_loop(1, W, greet, 0)
    def greet_sec(d, carry):
        pl.semaphore_signal(
            barrier, inc=1, device_id={"sec": lax.rem(s + d, SEC)}, device_id_type=MESH)
        return carry

    lax.fori_loop(1, SEC, greet_sec, 0)

    for copy in ints:
        copy.wait()
    chosen, ranks, owners, slots, count = [], [], [], [], jnp.int32(0)
    for k in range(NB):
        chosen.append(sel[0, k] != 0)
        owners.append(lax.div(tgt[0, k], NB))
        slots.append(lax.rem(tgt[0, k], NB))
        ranks.append(count)
        count = count + jnp.where(chosen[k], 1, 0)

    def block_of(i):
        found = jnp.int32(0)
        for k in range(NB):
            found = found + jnp.where(chosen[k] & (ranks[k] == i), k, 0)
        return found

    lane = lax.broadcasted_iota(jnp.int32, (1, 128), 1)
    message = jnp.zeros((1, 128), jnp.int32)
    for i in range(ITEMS):
        place = jnp.int32(-1)
        for k in range(NB):
            place = place + jnp.where(chosen[k] & (ranks[k] == i), tgt[0, k] + 1, 0)
        value = jnp.where(place >= 0, place * SUB + lane % SUB + 1, 0)
        message = jnp.where(lane // SUB == i, value, message)
    msend[...] = message
    mrecv[w] = message

    item_of, slot_of = [], []
    for t in range(SEC):
        item, slot = jnp.int32(0), jnp.int32(0)
        for k in range(NB):
            hit = chosen[k] & (owners[k] == t)
            item = item + jnp.where(hit, ranks[k], 0)
            slot = slot + jnp.where(hit, slots[k] + 1, 0)
        item_of.append(item)
        slot_of.append(slot)
        xmsend[t] = jnp.zeros((1, 128), jnp.int32) + slot
    xmrecv[s] = xmsend[s]

    pl.semaphore_wait(barrier, W - 1 + SEC - 1)

    def send_message(d, carry):
        pltpu.make_async_remote_copy(
            msend, mrecv.at[w], mesh_sems.at[0], mesh_sems.at[1],
            device_id={"term": z_peer(d)}, device_id_type=MESH).start()
        return carry

    lax.fori_loop(1, W, send_message, 0)

    def send_slot(d, carry):
        peer = lax.rem(s + d, SEC)
        pltpu.make_async_remote_copy(
            xmsend.at[peer], xmrecv.at[s], xs_sem.at[0], xr_sem.at[0],
            device_id={"sec": peer}, device_id_type=MESH).start()
        return carry

    lax.fori_loop(1, SEC, send_slot, 0)

    def wait_for(ref, sem):
        pltpu.make_async_copy(ref, ref, sem).wait()

    for copy in loads:
        copy.wait()

    row_id = lax.broadcasted_iota(jnp.int32, (BS, BS), 0)
    col_id = lax.broadcasted_iota(jnp.int32, (BS, BS), 1)

    def one_block(i):
        k = block_of(i)
        block = psi_v[k]
        keep = (row_id < dims[0, k]) & (col_id < dims[1, k])
        block = jnp.where(keep, block, jnp.zeros_like(block))
        half_product = jnp.dot(
            left_v[k].reshape(2 * BS, BS), block, preferred_element_type=jnp.float32
        ).astype(jnp.bfloat16)
        half_product = jnp.concatenate([half_product[:BS], half_product[BS:]], axis=1)
        total = jnp.dot(
            half_product, right_v[k].reshape(2 * BS, BS), preferred_element_type=jnp.float32)
        return total.reshape(W * G, SUB, BS)

    def one_pair(p, carry):
        both = []
        for e in range(2):
            block = one_block(2 * p + e)
            both.append(block)
            last = block.reshape(W, G, SUB, BS)[:, G - XG:, :, BS - COLS:]
            xitems[2 * p + e] = last.reshape(W * XG // 2, 2 * SUB, COLS).astype(jnp.bfloat16)
        both = jnp.concatenate(both, axis=1).astype(jnp.bfloat16).reshape(W, G, 2 * SUB, BS)
        part = pl.ds(pl.multiple_of(p * 2 * SUB, 2 * SUB), 2 * SUB)
        for c in range(C):
            at = c // G * COLS
            zsend[c, :, part, :] = both[:, c % G, :, at:at + COLS]

        def one(d, carry):
            peer = z_peer(d)
            pltpu.make_async_remote_copy(
                zsend.at[pl.ds(0, G), peer, part], zrecv.at[pl.ds(0, G), w, part],
                zs_sem.at[p], zr_sem.at[p],
                device_id={"term": peer}, device_id_type=MESH).start()
            return carry

        lax.fori_loop(1, W, one, 0)
        return carry

    lax.fori_loop(0, pairs, one_pair, 0)

    def send_chunk(c, carry):
        def one(d, carry):
            peer = z_peer(d)
            pltpu.make_async_remote_copy(
                zsend.at[c, peer], zrecv.at[c, w], zs_sem.at[pairs + c], zr_sem.at[pairs + c],
                device_id={"term": peer}, device_id_type=MESH).start()
            return carry

        return lax.fori_loop(1, W, one, carry)


    for t in range(SEC):
        xsend[t] = jnp.where(slot_of[t] > 0, xitems[item_of[t]], jnp.zeros(xsend.shape[1:], jnp.bfloat16))

    def send_item(d, carry):
        peer = lax.rem(s + d, SEC)
        pltpu.make_async_remote_copy(
            xsend.at[peer], xrecv.at[:, s], xs_sem.at[1], xr_sem.at[1],
            device_id={"sec": peer}, device_id_type=MESH).start()
        return carry

    lax.fori_loop(1, SEC, send_item, 0)
    lax.fori_loop(G, C, send_chunk, 0)
    xrecv[:, s] = xsend[s]
    for c in range(C):
        zrecv[c, w] = zsend[c, w]

    wait_for(xmrecv.at[pl.ds(0, SEC - 1)], xr_sem.at[0])
    wide = -(-SEC * 2 * SUB // 128)
    lane = lax.broadcasted_iota(jnp.int32, (1, wide * 128), 1)
    slot = jnp.zeros((1, wide * 128), jnp.int32)
    for n in range(SEC):
        slot = jnp.where(lane // (2 * SUB) == n, jnp.concatenate([xmrecv[n]] * wide, axis=1), slot)
    place = (slot - 1) * SUB + lane % (2 * SUB) // SUB * (NB * SUB) + lane % SUB
    place = jnp.where(slot > 0, place, -1)[:, :SEC * 2 * SUB]
    row = lax.broadcasted_iota(jnp.int32, xhot.shape, 0)
    xhot[...] = jnp.where(row == place, 1.0, 0.0).astype(jnp.bfloat16)

    wait_for(mrecv.at[pl.ds(0, W - 1)], mesh_sems.at[1])
    width = -(-K // 128) * 128
    places = jnp.zeros((2 * SUB, width), jnp.int32)
    for n in range(W):
        wide = jnp.broadcast_to(mrecv[n], (2 * SUB, 128))
        if width > 128:
            wide = jnp.concatenate([wide, jnp.zeros((2 * SUB, width - 128), jnp.int32)], axis=1)
        places = places + (pltpu.roll(wide, n * R6, 1) if n else wide)
    places = places[:, :K]
    step = lax.broadcasted_iota(jnp.int32, (2 * SUB, K), 0) + 1

    def fill(b, carry):
        first = pl.multiple_of(b * 2 * SUB, 2 * SUB)
        onehot[pl.ds(first, 2 * SUB), :] = jnp.where(
            places == step + first, 1.0, 0.0).astype(jnp.bfloat16)
        return carry

    lax.fori_loop(0, NY * NX * NB * SUB // (2 * SUB), fill, 0)

    block_rows = NX * NB * SUB

    def by_target(c):
        @pl.when(c == 0)
        def _():
            for p in range(pairs):
                part = pl.ds(p * 2 * SUB, 2 * SUB)
                wait_for(zrecv.at[pl.ds(0, G), pl.ds(0, W - 1), part], zr_sem.at[p])

        @pl.when(c >= G)
        def _():
            wait_for(zrecv.at[c, pl.ds(0, W - 1)], zr_sem.at[pairs + c])

        arrived = zrecv[c].reshape(K, COLS)
        for yy in range(NY):
            part = jnp.dot(
                onehot[yy * block_rows:(yy + 1) * block_rows, :], arrived,
                preferred_element_type=jnp.float32)
            ybuf[c, yy] = part.astype(jnp.bfloat16).reshape(NX, NB * SUB, COLS)
        for d in range(1, NY):
            yy = lax.rem(y + d, NY)
            pltpu.make_async_remote_copy(
                ybuf.at[c, yy, :, pl.ds(0, half)], a1.at[c, d - 1], s1_sem.at[0, c], r1_sem.at[0, c],
                device_id={"sec": sec_at(yy, x)}, device_id_type=MESH).start()
        for d in range(1, NX):
            xx = lax.rem(x + d, NX)
            pltpu.make_async_remote_copy(
                ybuf.at[c, :, xx, pl.ds(half, half)], b1.at[c, d - 1], s1_sem.at[1, c], r1_sem.at[1, c],
                device_id={"sec": sec_at(y, xx)}, device_id_type=MESH).start()

    def one_axis(c):
        wait_for(a1.at[c], r1_sem.at[0, c])
        total = ybuf[c, y, :, :half, :].astype(jnp.float32)
        for n in range(NY - 1):
            total = total + a1[c, n].astype(jnp.float32)
        a2s[c] = total.astype(jnp.bfloat16)
        for d in range(1, NX):
            xx = lax.rem(x + d, NX)
            pltpu.make_async_remote_copy(
                a2s.at[c, xx], a2.at[c, d - 1], s2_sem.at[0, c], r2_sem.at[0, c],
                device_id={"sec": sec_at(y, xx)}, device_id_type=MESH).start()
        wait_for(b1.at[c], r1_sem.at[1, c])
        total = ybuf[c, :, x, half:, :].astype(jnp.float32)
        for n in range(NX - 1):
            total = total + b1[c, n].astype(jnp.float32)
        b2s[c] = total.astype(jnp.bfloat16)
        for d in range(1, NY):
            yy = lax.rem(y + d, NY)
            pltpu.make_async_remote_copy(
                b2s.at[c, yy], b2.at[c, d - 1], s2_sem.at[1, c], r2_sem.at[1, c],
                device_id={"sec": sec_at(yy, x)}, device_id_type=MESH).start()

    def other_axis(c):
        wait_for(a2.at[c], r2_sem.at[0, c])
        wait_for(b2.at[c], r2_sem.at[1, c])
        for own, others, place, at in ((a2s, a2, x, 0), (b2s, b2, y, half)):
            total = own[c, place].astype(jnp.float32)
            for n in range(others.shape[1]):
                total = total + others[c, n].astype(jnp.float32)
            fin[c, at:at + half, :] = total

    def place_items():
        wait_for(xrecv.at[:, pl.ds(0, SEC - 1)], xr_sem.at[1])
        for n in range(W * XG // 2):
            part = jnp.dot(
                xhot[...], xrecv[n].reshape(SEC * 2 * SUB, COLS), preferred_element_type=jnp.float32
            ).astype(jnp.bfloat16)
            for e in range(2):
                at = 2 * n + e
                to, first = at // XG, at % XG * NB * SUB
                xplaced[to % 2, to // 2, first:first + NB * SUB, :] = part[e * NB * SUB:(e + 1) * NB * SUB]
        pltpu.make_async_remote_copy(
            xplaced.at[1 - core], xcore, xs_sem.at[2], xr_sem.at[2],
            device_id={"term": w + 1 - 2 * core}, device_id_type=MESH).start()

    def add_cores():
        wait_for(xcore, xr_sem.at[2])
        xsum[...] = (xplaced[core].astype(jnp.float32) + xcore[...].astype(jnp.float32)).astype(jnp.bfloat16)
        for d in range(1, W // 2):
            peer = lax.rem(z + d, W // 2)
            pltpu.make_async_remote_copy(
                xsum.at[peer], xlast.at[d - 1], xs_sem.at[3], xr_sem.at[3],
                device_id={"term": peer * 2 + core}, device_id_type=MESH).start()

    def step_of(t, carry):
        @pl.when(t == G + 1)
        def _():
            place_items()

        @pl.when(t == G + 2)
        def _():
            add_cores()

        @pl.when(t < C)
        def _():
            by_target(t)

        @pl.when((t >= 1) & (t <= C))
        def _():
            one_axis(t - 1)

        @pl.when(t >= 2)
        def _():
            other_axis(t - 2)

        return carry

    lax.fori_loop(0, C + 2, step_of, 0)

    wait_for(xlast, xr_sem.at[3])
    total = xsum[z].astype(jnp.float32)
    for n in range(W // 2 - 1):
        total = total + xlast[n].astype(jnp.float32)
    fin[C:] = total.reshape(XG, NB * SUB, COLS)

    row_id = lax.broadcasted_iota(jnp.int32, (rows, BS), 0) + w * rows
    col_id = lax.broadcasted_iota(jnp.int32, (rows, BS), 1)
    for j in range(NB):
        keep = (row_id < dims[0, j]) & (col_id < dims[1, j])
        total = jnp.concatenate([
            jnp.concatenate([
                fin[q * G + g, j * SUB:(j + 1) * SUB, :] for q in range(BS // COLS)], axis=1)
            for g in range(G)], axis=0)
        out[j] = jnp.where(keep, total, 0.0).astype(out.dtype)

    wait_for(mrecv.at[pl.ds(0, W - 1)], mesh_sems.at[0])
    for p in range(pairs):
        part = pl.ds(p * 2 * SUB, 2 * SUB)
        wait_for(zsend.at[pl.ds(0, G), pl.ds(0, W - 1), part], zs_sem.at[p])

    def sent(c, carry):
        @pl.when(c >= G)
        def _():
            wait_for(zsend.at[c, pl.ds(0, W - 1)], zs_sem.at[pairs + c])

        wait_for(a1.at[c], s1_sem.at[0, c])
        wait_for(b1.at[c], s1_sem.at[1, c])
        wait_for(a2.at[c], s2_sem.at[0, c])
        wait_for(b2.at[c], s2_sem.at[1, c])
        return carry

    lax.fori_loop(0, C, sent, 0)
    wait_for(xmrecv.at[pl.ds(0, SEC - 1)], xs_sem.at[0])
    wait_for(xsend.at[pl.ds(0, SEC - 1)], xs_sem.at[1])
    wait_for(xcore, xs_sem.at[2])
    wait_for(xlast, xs_sem.at[3])


def shards(W, SEC, psi, left_env, right_env, targets, selected, block_dims):
    NB, BS, _ = psi.shape
    NX = math.isqrt(SEC)
    NY = SEC // NX
    rows = BS // W
    C = BS // COLS * (rows // SUB) - XG
    pairs_here = W * XG // 2
    R6 = ITEMS * SUB
    half = NB * SUB // 2
    bf16, f32, i32 = jnp.bfloat16, jnp.float32, jnp.int32
    dma = pltpu.SemaphoreType.DMA
    hbm = pl.BlockSpec(memory_space=pltpu.HBM)
    return pl.pallas_call(
        functools.partial(kernel, W, NY, NX),
        out_shape=pltpu.VMEM((NB, rows, BS), bf16),
        in_specs=[hbm] * 6,
        out_specs=pl.BlockSpec(memory_space=pltpu.VMEM),
        scratch_shapes=[
            pltpu.SMEM((1, NB), i32),
            pltpu.SMEM((1, NB), i32),
            pltpu.SMEM((2, NB), i32),
            pltpu.VMEM((NB, BS, BS), bf16),
            pltpu.VMEM((NB, 2, BS, BS), bf16),
            pltpu.VMEM((NB, 2, BS, BS), bf16),
            pltpu.VMEM((C, W, R6, COLS), bf16),
            pltpu.VMEM((C, W, R6, COLS), bf16),
            pltpu.VMEM((1, 128), i32),
            pltpu.VMEM((W, 1, 128), i32),
            pltpu.VMEM((SEC * NB * SUB, W * R6), bf16),
            pltpu.VMEM((C, NY, NX, NB * SUB, COLS), bf16),
            pltpu.VMEM((C, NY - 1, NX, half, COLS), bf16),
            pltpu.VMEM((C, NX - 1, NY, half, COLS), bf16),
            pltpu.VMEM((C, NX, half, COLS), bf16),
            pltpu.VMEM((C, NY, half, COLS), bf16),
            pltpu.VMEM((C, NX - 1, half, COLS), bf16),
            pltpu.VMEM((C, NY - 1, half, COLS), bf16),
            pltpu.VMEM((C + XG, NB * SUB, COLS), f32),
            pltpu.VMEM((SEC, 1, 128), i32),
            pltpu.VMEM((SEC, 1, 128), i32),
            pltpu.VMEM((ITEMS, pairs_here, 2 * SUB, COLS), bf16),
            pltpu.VMEM((SEC, pairs_here, 2 * SUB, COLS), bf16),
            pltpu.VMEM((pairs_here, SEC, 2 * SUB, COLS), bf16),
            pltpu.VMEM((2 * NB * SUB, SEC * 2 * SUB), bf16),
            pltpu.VMEM((2, W // 2, XG * NB * SUB, COLS), bf16),
            pltpu.VMEM((W // 2, XG * NB * SUB, COLS), bf16),
            pltpu.VMEM((W // 2, XG * NB * SUB, COLS), bf16),
            pltpu.VMEM((W // 2 - 1, XG * NB * SUB, COLS), bf16),
            dma((3,)), dma((5,)), dma((2,)), dma((ITEMS // 2 + C,)), dma((ITEMS // 2 + C,)),
            dma((2, C)), dma((2, C)), dma((2, C)), dma((2, C)), dma((4,)), dma((4,)),
        ],
        compiler_params=pltpu.CompilerParams(
            collective_id=0, has_side_effects=True, vmem_limit_bytes=54 * 2**20),
        cost_estimate=pl.CostEstimate(flops=8 * 10**9, bytes_accessed=12 * 10**6, transcendentals=0),
        name="davidson",
    )(targets, selected, block_dims.T, psi, left_env, right_env)


def solution(mesh):
    W, SEC = mesh.shape["term"], mesh.shape["sec"]
    return jax.shard_map(
        functools.partial(shards, W, SEC),
        mesh=mesh,
        in_specs=(
            P("sec", None, None),
            P("term", None, "sec", None, None),
            P("term", None, "sec", None, None),
            P("term", "sec"),
            P("term", "sec"),
            P("sec", None),
        ),
        out_specs=P("sec", "term", None),
        check_vma=False,
    )
```

time: 69.6 us -> 56.1 us (0.81)
  the two profiles are of different devices: /device:TPU:1 before, /device:TPU:2 now
where the time goes in v2:
time: 56.1 us
  Pallas kernels  55.4 us (99%)
  local copies, waits for them, and re-layouts  0.66 us (1%)
    pallas_call x1, Pallas kernels, shards(): pl.pallas_call(functools.partial(kernel, W, NY, NX), out_shape=pltpu.VMEM...  55.4 us

profile of v2, /device:TPU:2, one launch (start us, length us, event | category | flops | bytes accessed | tf_op | source)
XLA Modules:
  0.0 56.1 jit_solution(17326796735907381193)
XLA Ops:
  0.0 55.4 %davidson.1 = bf16[8,24,384]{2,1,0:T(8,128)(2,1)S(1)} custom-call(s32[1,8]{1,0:T(1,128)} %tgt_h.1, s32[1,8]{1,0:T(1,128)} %sel_h.1, s32[2,8]{1,0:T(2,128)} %bitcast.1, bf16[8,384,384]{2,1,0:T(8,128)(2,1)} %psi_h.1, bf16[1,2,8,384,384]{4,3,2,1,0:T(8,128)(2,1)} %left_h.1, bf16[1,2,8,384,384]{4,3,2,1,0:T(8,128)(2,1)} %right_h.1), custom_call_target="tpu_custom_call" | custom-call | flops 8000000000 | bytes 12000000 | tf_op jit(solution)/shard_map/davidson/pallas_call | solution.py:396
  55.4 0.7 %copy.8 = bf16[8,24,384]{2,1,0:T(8,128)(2,1)} copy(bf16[8,24,384]{2,1,0:T(8,128)(2,1)S(1)} %davidson.1) | data formatting | bytes 294912

commit v3 on v2

--- a/solution.py
+++ b/solution.py
@@ -18,10 +18,10 @@
 def kernel(
     W, NY, NX,
     tgt_h, sel_h, dims_h, psi_h, left_h, right_h, out,
-    tgt, sel, dims, psi_v, left_v, right_v, zsend, zrecv, msend, mrecv, onehot, ybuf,
+    tgt, sel, dims, psi_v, left_v, right_v, rest_v, halves, zsend, zrecv, msend, mrecv, onehot, ybuf,
     a1, b1, a2s, b2s, a2, b2, fin,
-    xmsend, xmrecv, xitems, xsend, xrecv, xhot, xplaced, xcore, xsum, xlast,
-    int_sem, load_sem, mesh_sems, zs_sem, zr_sem, s1_sem, r1_sem, s2_sem, r2_sem, xs_sem, xr_sem,
+    direct, xmsend, xmrecv, xitems, xsend, xrecv, xhot, xplaced, xcore, xsum, xlast,
+    int_sem, load_sem, mesh_sems, zs_sem, zr_sem, s1_sem, r1_sem, s2_sem, r2_sem, xs_sem, xr_sem, d_sem,
 ):
     w = lax.axis_index("term")
     s = lax.axis_index("sec")
@@ -45,13 +45,23 @@
     for m in range(2):
         loads.append((left_h.at[0, m], left_v.at[:, m]))
     for m in range(2):
-        loads.append((right_h.at[0, m], right_v.at[:, m]))
+        loads.append((right_h.at[0, m, :, :, pl.ds(0, COLS)], right_v.at[:, m]))
+    for m in range(2):
+        loads.append((right_h.at[0, m, :, :, pl.ds(COLS, BS - COLS)], rest_v.at[:, m]))
     loads = [pltpu.make_async_copy(a, b, load_sem.at[n]) for n, (a, b) in enumerate(loads)]
-    for copy in loads:
+    for copy in loads[:5]:
         copy.start()
 
     def z_peer(d):
         return lax.rem(w + d, W)
+
+    def far(d, n):
+        return -min(d, n - d)
+
+    z_turns = sorted(((d, c) for d in range(1, W // 2) for c in range(2)), key=lambda t: far(t[0], W // 2))
+    z_turns = [(0, 1)] + z_turns
+    turns = [(dy, dx) for dy in range(NY) for dx in range(NX) if dy or dx]
+    turns = sorted(turns, key=lambda t: far(t[0], NY) + far(t[1], NX))
 
     def sec_at(yy, xx):
         return yy * NX + xx
@@ -109,15 +119,12 @@
         xmsend[t] = jnp.zeros((1, 128), jnp.int32) + slot
     xmrecv[s] = xmsend[s]
 
-    pl.semaphore_wait(barrier, W - 1 + SEC - 1)
-
     def send_message(d, carry):
         pltpu.make_async_remote_copy(
             msend, mrecv.at[w], mesh_sems.at[0], mesh_sems.at[1],
             device_id={"term": z_peer(d)}, device_id_type=MESH).start()
         return carry
 
-    lax.fori_loop(1, W, send_message, 0)
 
     def send_slot(d, carry):
         peer = lax.rem(s + d, SEC)
@@ -126,18 +133,19 @@
             device_id={"sec": peer}, device_id_type=MESH).start()
         return carry
 
-    lax.fori_loop(1, SEC, send_slot, 0)
 
     def wait_for(ref, sem):
         pltpu.make_async_copy(ref, ref, sem).wait()
 
-    for copy in loads:
+    for copy in loads[:5]:
         copy.wait()
+    for copy in loads[5:]:
+        copy.start()
 
     row_id = lax.broadcasted_iota(jnp.int32, (BS, BS), 0)
     col_id = lax.broadcasted_iota(jnp.int32, (BS, BS), 1)
 
-    def one_block(i):
+    def first_columns(i):
         k = block_of(i)
         block = psi_v[k]
         keep = (row_id < dims[0, k]) & (col_id < dims[1, k])
@@ -146,22 +154,39 @@
             left_v[k].reshape(2 * BS, BS), block, preferred_element_type=jnp.float32
         ).astype(jnp.bfloat16)
         half_product = jnp.concatenate([half_product[:BS], half_product[BS:]], axis=1)
+        halves[i] = half_product
         total = jnp.dot(
-            half_product, right_v[k].reshape(2 * BS, BS), preferred_element_type=jnp.float32)
-        return total.reshape(W * G, SUB, BS)
-
-    def one_pair(p, carry):
-        both = []
-        for e in range(2):
-            block = one_block(2 * p + e)
-            both.append(block)
-            last = block.reshape(W, G, SUB, BS)[:, G - XG:, :, BS - COLS:]
-            xitems[2 * p + e] = last.reshape(W * XG // 2, 2 * SUB, COLS).astype(jnp.bfloat16)
-        both = jnp.concatenate(both, axis=1).astype(jnp.bfloat16).reshape(W, G, 2 * SUB, BS)
-        part = pl.ds(pl.multiple_of(p * 2 * SUB, 2 * SUB), 2 * SUB)
-        for c in range(C):
-            at = c // G * COLS
-            zsend[c, :, part, :] = both[:, c % G, :, at:at + COLS]
+            half_product, right_v[k].reshape(2 * BS, COLS), preferred_element_type=jnp.float32)
+        return total.reshape(W * G, SUB, COLS)
+
+    def other_columns(i):
+        k = block_of(i)
+        total = jnp.dot(
+            halves[i], rest_v[k].reshape(2 * BS, BS - COLS), preferred_element_type=jnp.float32)
+        last = total.reshape(W, G, SUB, BS - COLS)[:, G - XG:, :, BS - 2 * COLS:]
+        xitems[i] = last.reshape(W * XG // 2, 2 * SUB, COLS).astype(jnp.bfloat16)
+        return total.reshape(W * G, SUB, BS - COLS)
+
+    def rows_of(p):
+        return pl.ds(pl.multiple_of(p * 2 * SUB, 2 * SUB), 2 * SUB)
+
+    def first_pair(p):
+        both = [first_columns(2 * p), first_columns(2 * p + 1)]
+        both = jnp.concatenate(both, axis=1).astype(jnp.bfloat16).reshape(W, G, 2 * SUB, COLS)
+        for c in range(G):
+            zsend[c, :, rows_of(p), :] = both[:, c]
+
+    def other_pair(p, carry):
+        both = [other_columns(2 * p), other_columns(2 * p + 1)]
+        both = jnp.concatenate(both, axis=1).astype(jnp.bfloat16)
+        both = both.reshape(W, G, 2 * SUB, BS - COLS)
+        for c in range(G, C):
+            at = (c // G - 1) * COLS
+            zsend[c, :, rows_of(p), :] = both[:, c % G, :, at:at + COLS]
+        return carry
+
+    def send_pair(p):
+        part = rows_of(p)
 
         def one(d, carry):
             peer = z_peer(d)
@@ -172,32 +197,39 @@
             return carry
 
         lax.fori_loop(1, W, one, 0)
-        return carry
-
-    lax.fori_loop(0, pairs, one_pair, 0)
+
+    def next_pair(p, carry):
+        first_pair(p)
+        send_pair(p)
+        return carry
+
+    first_pair(0)
+    pl.semaphore_wait(barrier, W - 1 + SEC - 1)
+    send_pair(0)
+    lax.fori_loop(1, W, send_message, 0)
+    lax.fori_loop(1, SEC, send_slot, 0)
+    lax.fori_loop(1, pairs, next_pair, 0)
+    for copy in loads[5:]:
+        copy.wait()
+    lax.fori_loop(0, pairs, other_pair, 0)
 
     def send_chunk(c, carry):
-        def one(d, carry):
-            peer = z_peer(d)
+        for dz, dc in z_turns:
+            peer = lax.rem(z + dz, W // 2) * 2 + lax.rem(core + dc, 2)
             pltpu.make_async_remote_copy(
                 zsend.at[c, peer], zrecv.at[c, w], zs_sem.at[pairs + c], zr_sem.at[pairs + c],
                 device_id={"term": peer}, device_id_type=MESH).start()
-            return carry
-
-        return lax.fori_loop(1, W, one, carry)
+        return carry
 
 
     for t in range(SEC):
         xsend[t] = jnp.where(slot_of[t] > 0, xitems[item_of[t]], jnp.zeros(xsend.shape[1:], jnp.bfloat16))
 
-    def send_item(d, carry):
-        peer = lax.rem(s + d, SEC)
+    for dy, dx in turns:
+        peer = sec_at(lax.rem(y + dy, NY), lax.rem(x + dx, NX))
         pltpu.make_async_remote_copy(
             xsend.at[peer], xrecv.at[:, s], xs_sem.at[1], xr_sem.at[1],
             device_id={"sec": peer}, device_id_type=MESH).start()
-        return carry
-
-    lax.fori_loop(1, SEC, send_item, 0)
     lax.fori_loop(G, C, send_chunk, 0)
     xrecv[:, s] = xsend[s]
     for c in range(C):
@@ -262,6 +294,29 @@
             pltpu.make_async_remote_copy(
                 ybuf.at[c, :, xx, pl.ds(half, half)], b1.at[c, d - 1], s1_sem.at[1, c], r1_sem.at[1, c],
                 device_id={"sec": sec_at(y, xx)}, device_id_type=MESH).start()
+
+    def by_target_at_once(c):
+        wait_for(zrecv.at[c, pl.ds(0, W - 1)], zr_sem.at[pairs + c])
+        arrived = zrecv[c].reshape(K, COLS)
+        for dy in sorted(range(NY), key=lambda d: far(d, NY)):
+            yy = lax.rem(y + dy, NY)
+            first = pl.multiple_of(yy * block_rows, block_rows)
+            part = jnp.dot(
+                onehot[pl.ds(first, block_rows), :], arrived, preferred_element_type=jnp.float32)
+            ybuf[c, yy] = part.astype(jnp.bfloat16).reshape(NX, NB * SUB, COLS)
+            for dx in sorted(range(NX), key=lambda d: far(d, NX)):
+                if dx or dy:
+                    xx = lax.rem(x + dx, NX)
+                    pltpu.make_async_remote_copy(
+                        ybuf.at[c, yy, xx], direct.at[dy * NX + dx - 1], d_sem.at[0], d_sem.at[1],
+                        device_id={"sec": sec_at(yy, xx)}, device_id_type=MESH).start()
+
+    def add_direct(c):
+        wait_for(direct, d_sem.at[1])
+        total = ybuf[c, y, x].astype(jnp.float32)
+        for n in range(SEC - 1):
+            total = total + direct[n].astype(jnp.float32)
+        fin[c] = total
 
     def one_axis(c):
         wait_for(a1.at[c], r1_sem.at[0, c])
@@ -318,19 +373,23 @@
                 device_id={"term": peer * 2 + core}, device_id_type=MESH).start()
 
     def step_of(t, carry):
+        @pl.when(t == G)
+        def _():
+            place_items()
+
         @pl.when(t == G + 1)
         def _():
-            place_items()
-
-        @pl.when(t == G + 2)
-        def _():
             add_cores()
 
-        @pl.when(t < C)
+        @pl.when(t < C - 1)
         def _():
             by_target(t)
 
-        @pl.when((t >= 1) & (t <= C))
+        @pl.when(t == C - 1)
+        def _():
+            by_target_at_once(C - 1)
+
+        @pl.when((t >= 1) & (t < C))
         def _():
             one_axis(t - 1)
 
@@ -340,7 +399,8 @@
 
         return carry
 
-    lax.fori_loop(0, C + 2, step_of, 0)
+    lax.fori_loop(0, C + 1, step_of, 0)
+    add_direct(C - 1)
 
     wait_for(xlast, xr_sem.at[3])
     total = xsum[z].astype(jnp.float32)
@@ -368,13 +428,17 @@
         def _():
             wait_for(zsend.at[c, pl.ds(0, W - 1)], zs_sem.at[pairs + c])
 
-        wait_for(a1.at[c], s1_sem.at[0, c])
-        wait_for(b1.at[c], s1_sem.at[1, c])
-        wait_for(a2.at[c], s2_sem.at[0, c])
-        wait_for(b2.at[c], s2_sem.at[1, c])
+        @pl.when(c < C - 1)
+        def _():
+            wait_for(a1.at[c], s1_sem.at[0, c])
+            wait_for(b1.at[c], s1_sem.at[1, c])
+            wait_for(a2.at[c], s2_sem.at[0, c])
+            wait_for(b2.at[c], s2_sem.at[1, c])
+
         return carry
 
     lax.fori_loop(0, C, sent, 0)
+    wait_for(direct, d_sem.at[0])
     wait_for(xmrecv.at[pl.ds(0, SEC - 1)], xs_sem.at[0])
     wait_for(xsend.at[pl.ds(0, SEC - 1)], xs_sem.at[1])
     wait_for(xcore, xs_sem.at[2])
@@ -404,20 +468,23 @@
             pltpu.SMEM((2, NB), i32),
             pltpu.VMEM((NB, BS, BS), bf16),
             pltpu.VMEM((NB, 2, BS, BS), bf16),
-            pltpu.VMEM((NB, 2, BS, BS), bf16),
+            pltpu.VMEM((NB, 2, BS, COLS), bf16),
+            pltpu.VMEM((NB, 2, BS, BS - COLS), bf16),
+            pltpu.VMEM((ITEMS, BS, 2 * BS), bf16),
             pltpu.VMEM((C, W, R6, COLS), bf16),
             pltpu.VMEM((C, W, R6, COLS), bf16),
             pltpu.VMEM((1, 128), i32),
             pltpu.VMEM((W, 1, 128), i32),
             pltpu.VMEM((SEC * NB * SUB, W * R6), bf16),
             pltpu.VMEM((C, NY, NX, NB * SUB, COLS), bf16),
-            pltpu.VMEM((C, NY - 1, NX, half, COLS), bf16),
-            pltpu.VMEM((C, NX - 1, NY, half, COLS), bf16),
-            pltpu.VMEM((C, NX, half, COLS), bf16),
-            pltpu.VMEM((C, NY, half, COLS), bf16),
-            pltpu.VMEM((C, NX - 1, half, COLS), bf16),
-            pltpu.VMEM((C, NY - 1, half, COLS), bf16),
+            pltpu.VMEM((C - 1, NY - 1, NX, half, COLS), bf16),
+            pltpu.VMEM((C - 1, NX - 1, NY, half, COLS), bf16),
+            pltpu.VMEM((C - 1, NX, half, COLS), bf16),
+            pltpu.VMEM((C - 1, NY, half, COLS), bf16),
+            pltpu.VMEM((C - 1, NX - 1, half, COLS), bf16),
+            pltpu.VMEM((C - 1, NY - 1, half, COLS), bf16),
             pltpu.VMEM((C + XG, NB * SUB, COLS), f32),
+            pltpu.VMEM((SEC - 1, NB * SUB, COLS), bf16),
             pltpu.VMEM((SEC, 1, 128), i32),
             pltpu.VMEM((SEC, 1, 128), i32),
             pltpu.VMEM((ITEMS, pairs_here, 2 * SUB, COLS), bf16),
@@ -428,8 +495,8 @@
             pltpu.VMEM((W // 2, XG * NB * SUB, COLS), bf16),
             pltpu.VMEM((W // 2, XG * NB * SUB, COLS), bf16),
             pltpu.VMEM((W // 2 - 1, XG * NB * SUB, COLS), bf16),
-            dma((3,)), dma((5,)), dma((2,)), dma((ITEMS // 2 + C,)), dma((ITEMS // 2 + C,)),
-            dma((2, C)), dma((2, C)), dma((2, C)), dma((2, C)), dma((4,)), dma((4,)),
+            dma((3,)), dma((7,)), dma((2,)), dma((ITEMS // 2 + C,)), dma((ITEMS // 2 + C,)),
+            dma((2, C - 1)), dma((2, C - 1)), dma((2, C - 1)), dma((2, C - 1)), dma((4,)), dma((4,)), dma((2,)),
         ],
         compiler_params=pltpu.CompilerParams(
             collective_id=0, has_side_effects=True, vmem_limit_bytes=54 * 2**20),

time: 56.1 us -> 52.1 us (0.929)
  the two profiles are of different devices: /device:TPU:2 before, /device:TPU:1 now
where the time goes in v3:
time: 52.1 us; the launch traced here: 51.9 us
  Pallas kernels  51.2 us (98%)
  local copies, waits for them, and re-layouts  0.66 us (1%)
    pallas_call x1, Pallas kernels, shards(): pl.pallas_call(functools.partial(kernel, W, NY, NX), out_shape=pltpu.VMEM...  51.2 us

profile of v3, /device:TPU:1, one launch (start us, length us, event | category | flops | bytes accessed | tf_op | source)
XLA Modules:
  0.0 51.9 jit_solution(4002839886842338594)
XLA Ops:
  0.0 51.2 %davidson.1 = bf16[8,24,384]{2,1,0:T(8,128)(2,1)S(1)} custom-call(s32[1,8]{1,0:T(1,128)} %tgt_h.1, s32[1,8]{1,0:T(1,128)} %sel_h.1, s32[2,8]{1,0:T(2,128)} %bitcast.1, bf16[8,384,384]{2,1,0:T(8,128)(2,1)} %psi_h.1, bf16[1,2,8,384,384]{4,3,2,1,0:T(8,128)(2,1)} %left_h.1, bf16[1,2,8,384,384]{4,3,2,1,0:T(8,128)(2,1)} %right_h.1), custom_call_target="tpu_custom_call" | custom-call | flops 8000000000 | bytes 12000000 | tf_op jit(solution)/shard_map/davidson/pallas_call | solution.py:460
  51.2 0.7 %copy.8 = bf16[8,24,384]{2,1,0:T(8,128)(2,1)} copy(bf16[8,24,384]{2,1,0:T(8,128)(2,1)S(1)} %davidson.1) | data formatting | bytes 294912

commit v4 on v3

--- a/solution.py
+++ b/solution.py
@@ -159,13 +159,10 @@
             half_product, right_v[k].reshape(2 * BS, COLS), preferred_element_type=jnp.float32)
         return total.reshape(W * G, SUB, COLS)
 
-    def other_columns(i):
-        k = block_of(i)
-        total = jnp.dot(
-            halves[i], rest_v[k].reshape(2 * BS, BS - COLS), preferred_element_type=jnp.float32)
-        last = total.reshape(W, G, SUB, BS - COLS)[:, G - XG:, :, BS - 2 * COLS:]
-        xitems[i] = last.reshape(W * XG // 2, 2 * SUB, COLS).astype(jnp.bfloat16)
-        return total.reshape(W * G, SUB, BS - COLS)
+    def other_columns(i, first, width):
+        side = rest_v[block_of(i), :, :, first - COLS:first - COLS + width].reshape(2 * BS, width)
+        total = jnp.dot(halves[i], side, preferred_element_type=jnp.float32)
+        return total.reshape(W * G, SUB, width)
 
     def rows_of(p):
         return pl.ds(pl.multiple_of(p * 2 * SUB, 2 * SUB), 2 * SUB)
@@ -176,13 +173,25 @@
         for c in range(G):
             zsend[c, :, rows_of(p), :] = both[:, c]
 
-    def other_pair(p, carry):
-        both = [other_columns(2 * p), other_columns(2 * p + 1)]
-        both = jnp.concatenate(both, axis=1).astype(jnp.bfloat16)
-        both = both.reshape(W, G, 2 * SUB, BS - COLS)
-        for c in range(G, C):
-            at = (c // G - 1) * COLS
+    def put(p, both, first, width):
+        both = jnp.concatenate(both, axis=1).astype(jnp.bfloat16).reshape(W, G, 2 * SUB, width)
+        for c in range(first // COLS * G, min(C, (first + width) // COLS * G)):
+            at = c // G * COLS - first
             zsend[c, :, rows_of(p), :] = both[:, c % G, :, at:at + COLS]
+
+    def last_pair(p, carry):
+        both = []
+        for e in range(2):
+            total = other_columns(2 * p + e, BS - COLS, COLS)
+            both.append(total)
+            last = total.reshape(W, G, SUB, COLS)[:, G - XG:]
+            xitems[2 * p + e] = last.reshape(W * XG // 2, 2 * SUB, COLS).astype(jnp.bfloat16)
+        put(p, both, BS - COLS, COLS)
+        return carry
+
+    def middle_pair(p, carry):
+        width = BS - 2 * COLS
+        put(p, [other_columns(2 * p + e, COLS, width) for e in range(2)], COLS, width)
         return carry
 
     def send_pair(p):
@@ -211,7 +220,7 @@
     lax.fori_loop(1, pairs, next_pair, 0)
     for copy in loads[5:]:
         copy.wait()
-    lax.fori_loop(0, pairs, other_pair, 0)
+    lax.fori_loop(0, pairs, last_pair, 0)
 
     def send_chunk(c, carry):
         for dz, dc in z_turns:
@@ -230,6 +239,8 @@
         pltpu.make_async_remote_copy(
             xsend.at[peer], xrecv.at[:, s], xs_sem.at[1], xr_sem.at[1],
             device_id={"sec": peer}, device_id_type=MESH).start()
+    if BS > 2 * COLS:
+        lax.fori_loop(0, pairs, middle_pair, 0)
     lax.fori_loop(G, C, send_chunk, 0)
     xrecv[:, s] = xsend[s]
     for c in range(C):

time: 52.1 us -> 52.1 us (level)
  no operation moved by 1% of the time
where the time goes in v4:
time: 52.1 us; the launch traced here: 51.9 us
  Pallas kernels  51.2 us (98%)
  local copies, waits for them, and re-layouts  0.66 us (1%)
    pallas_call x1, Pallas kernels, shards(): pl.pallas_call(functools.partial(kernel, W, NY, NX), out_shape=pltpu.VMEM...  51.2 us

profile of v4, /device:TPU:1, one launch (start us, length us, event | category | flops | bytes accessed | tf_op | source)
XLA Modules:
  0.0 51.9 jit_solution(7061983209795242554)
XLA Ops:
  0.0 51.2 %davidson.1 = bf16[8,24,384]{2,1,0:T(8,128)(2,1)S(1)} custom-call(s32[1,8]{1,0:T(1,128)} %tgt_h.1, s32[1,8]{1,0:T(1,128)} %sel_h.1, s32[2,8]{1,0:T(2,128)} %bitcast.1, bf16[8,384,384]{2,1,0:T(8,128)(2,1)} %psi_h.1, bf16[1,2,8,384,384]{4,3,2,1,0:T(8,128)(2,1)} %left_h.1, bf16[1,2,8,384,384]{4,3,2,1,0:T(8,128)(2,1)} %right_h.1), custom_call_target="tpu_custom_call" | custom-call | flops 8000000000 | bytes 12000000 | tf_op jit(solution)/shard_map/davidson/pallas_call | solution.py:471
  51.2 0.7 %copy.8 = bf16[8,24,384]{2,1,0:T(8,128)(2,1)} copy(bf16[8,24,384]{2,1,0:T(8,128)(2,1)S(1)} %davidson.1) | data formatting | bytes 294912

commit v5 on v3

--- a/solution.py
+++ b/solution.py
@@ -284,12 +284,12 @@
                 onehot[yy * block_rows:(yy + 1) * block_rows, :], arrived,
                 preferred_element_type=jnp.float32)
             ybuf[c, yy] = part.astype(jnp.bfloat16).reshape(NX, NB * SUB, COLS)
-        for d in range(1, NY):
+        for d in sorted(range(1, NY), key=lambda d: far(d, NY)):
             yy = lax.rem(y + d, NY)
             pltpu.make_async_remote_copy(
                 ybuf.at[c, yy, :, pl.ds(0, half)], a1.at[c, d - 1], s1_sem.at[0, c], r1_sem.at[0, c],
                 device_id={"sec": sec_at(yy, x)}, device_id_type=MESH).start()
-        for d in range(1, NX):
+        for d in sorted(range(1, NX), key=lambda d: far(d, NX)):
             xx = lax.rem(x + d, NX)
             pltpu.make_async_remote_copy(
                 ybuf.at[c, :, xx, pl.ds(half, half)], b1.at[c, d - 1], s1_sem.at[1, c], r1_sem.at[1, c],
@@ -324,7 +324,7 @@
         for n in range(NY - 1):
             total = total + a1[c, n].astype(jnp.float32)
         a2s[c] = total.astype(jnp.bfloat16)
-        for d in range(1, NX):
+        for d in sorted(range(1, NX), key=lambda d: far(d, NX)):
             xx = lax.rem(x + d, NX)
             pltpu.make_async_remote_copy(
                 a2s.at[c, xx], a2.at[c, d - 1], s2_sem.at[0, c], r2_sem.at[0, c],
@@ -334,7 +334,7 @@
         for n in range(NX - 1):
             total = total + b1[c, n].astype(jnp.float32)
         b2s[c] = total.astype(jnp.bfloat16)
-        for d in range(1, NY):
+        for d in sorted(range(1, NY), key=lambda d: far(d, NY)):
             yy = lax.rem(y + d, NY)
             pltpu.make_async_remote_copy(
                 b2s.at[c, yy], b2.at[c, d - 1], s2_sem.at[1, c], r2_sem.at[1, c],
@@ -366,7 +366,7 @@
     def add_cores():
         wait_for(xcore, xr_sem.at[2])
         xsum[...] = (xplaced[core].astype(jnp.float32) + xcore[...].astype(jnp.float32)).astype(jnp.bfloat16)
-        for d in range(1, W // 2):
+        for d in sorted(range(1, W // 2), key=lambda d: far(d, W // 2)):
             peer = lax.rem(z + d, W // 2)
             pltpu.make_async_remote_copy(
                 xsum.at[peer], xlast.at[d - 1], xs_sem.at[3], xr_sem.at[3],

time: 52.1 us -> 52.5 us (level)
  Pallas kernels: 51.2 us -> 51.8 us
where the time goes in v5:
time: 52.5 us; the launch traced here: 52.4 us
  Pallas kernels  51.8 us (99%)
  local copies, waits for them, and re-layouts  0.66 us (1%)
    pallas_call x1, Pallas kernels, shards(): pl.pallas_call(functools.partial(kernel, W, NY, NX), out_shape=pltpu.VMEM...  51.8 us

profile of v5, /device:TPU:1, one launch (start us, length us, event | category | flops | bytes accessed | tf_op | source)
XLA Modules:
  0.0 52.4 jit_solution(17922669020798441566)
XLA Ops:
  0.0 51.8 %davidson.1 = bf16[8,24,384]{2,1,0:T(8,128)(2,1)S(1)} custom-call(s32[1,8]{1,0:T(1,128)} %tgt_h.1, s32[1,8]{1,0:T(1,128)} %sel_h.1, s32[2,8]{1,0:T(2,128)} %bitcast.1, bf16[8,384,384]{2,1,0:T(8,128)(2,1)} %psi_h.1, bf16[1,2,8,384,384]{4,3,2,1,0:T(8,128)(2,1)} %left_h.1, bf16[1,2,8,384,384]{4,3,2,1,0:T(8,128)(2,1)} %right_h.1), custom_call_target="tpu_custom_call" | custom-call | flops 8000000000 | bytes 12000000 | tf_op jit(solution)/shard_map/davidson/pallas_call | solution.py:460
  51.8 0.7 %copy.8 = bf16[8,24,384]{2,1,0:T(8,128)(2,1)} copy(bf16[8,24,384]{2,1,0:T(8,128)(2,1)S(1)} %davidson.1) | data formatting | bytes 294912
